TPU v7x, 32 devices: a whole 2x2x4 slice. The times are simulated.
32 devices in a mesh: gx: 8 (over y, x, core), gy: 4 (over z).
Axes of the slice: x: 2, y: 2, z: 4, core: 2. Of those that a mesh axis runs over, the one named last changes fastest.
Arguments:
- velocity: float32 [3, 64, 128, 128], P(None, 'gx', 'gy'), may hold values from -6 to 6
- forcing: float32 [3, 64, 128, 128], P(None, 'gx', 'gy'), may hold values from -6 to 6
- viscosity: float32 [64, 128, 128], P('gx', 'gy'), may hold values from 0.1 to 2
- multipliers: float32 [8, 4, 8, 3, 384], P('gx', 'gy'), may hold values from -4 to 4
- sphere_centres: int32 [8, 4, 8, 3], P('gx', 'gy'), may hold values from 0 to 119, as said below
- sphere_offsets: int32 [8, 4, 8, 3, 384], P('gx', 'gy'), may hold values from -8 to 8, as said below
- sphere_count: int32 [8, 4], P('gx', 'gy'), may hold values from 1 to 8, as said below
Outputs:
- velocity_out: float32 [3, 64, 128, 128], P(None, 'gx', 'gy')
- body_motion: float32 [8, 4, 8, 6], P('gx', 'gy')
Inputs may be any that keep to these rules, and one draw needn't show every extreme that they name: `sphere_centres`: the first two coordinates of a slot's centre lie in its owner's block, 0 to 7 and 0 to 31, the third lies in 8 to 119; some slot reaches each end. `sphere_offsets`: every point lies at a distance between 7 and 8 from its sphere's centre. Slots 0 to sphere_count - 1 of a device hold spheres, the others are empty; in every draw some device fills all 8 slots and some device has one sphere.
All inputs are finite; a program needn't handle non-finite values.
Results may differ from a plain program's by a relative error of at most 0.0001.
Values sent between devices are 32-bit elements; how exact they have to be, the bound alone decides.
A program may use at most 128 MiB of HBM per device.

v0:
```python
import jax
import jax.numpy as jnp
from jax import lax
from jax.sharding import PartitionSpec as P

SWEEPS = 4
UZ = 3


MASS_TERM = 0.2
VERTICAL_WEIGHT = 0.25
UZAWA_STEP = 0.5


def extended(block, sides, width):
    for axis, dim in sides:
        count = lax.axis_size(axis)
        forward = [(i, i + 1) for i in range(count - 1)]
        forward.append((count - 1, 0))
        backward = [(target, source) for source, target in forward]
        low = lax.ppermute(
            lax.slice_in_dim(block, block.shape[dim] - width, None, axis=dim), axis, forward
        )
        high = lax.ppermute(lax.slice_in_dim(block, 0, width, axis=dim), axis, backward)
        block = jnp.concatenate([low, block, high], axis=dim)
    return block


def cross_product(left, right):
    return jnp.stack(
        [
            left[..., 1, :] * right[..., 2, :] - left[..., 2, :] * right[..., 1, :],
            left[..., 2, :] * right[..., 0, :] - left[..., 0, :] * right[..., 2, :],
            left[..., 0, :] * right[..., 1, :] - left[..., 1, :] * right[..., 0, :],
        ],
        -2,
    )


def face_terms(viscous):
    centre = viscous[1:-1, 1:-1, :]
    vertical = jnp.concatenate([viscous[:, :, :1], viscous, viscous[:, :, -1:]], axis=2)
    k_west = 0.5 * (centre + viscous[:-2, 1:-1, :])
    k_east = 0.5 * (centre + viscous[2:, 1:-1, :])
    k_south = 0.5 * (centre + viscous[1:-1, :-2, :])
    k_north = 0.5 * (centre + viscous[1:-1, 2:, :])
    k_below = VERTICAL_WEIGHT * 0.5 * (centre + vertical[1:-1, 1:-1, :-2])
    k_above = VERTICAL_WEIGHT * 0.5 * (centre + vertical[1:-1, 1:-1, 2:])
    inverse = 1.0 / (MASS_TERM + k_west + k_east + k_south + k_north + k_below + k_above)
    return (k_west, k_east, k_south, k_north, k_below, k_above, inverse)


def jacobi_step(padded, terms, source):
    k_west, k_east, k_south, k_north, k_below, k_above, inverse = terms
    interior = padded[..., 1:-1, 1:-1, :]
    zero_plane = jnp.zeros(interior.shape[:-1] + (1,), interior.dtype)
    column_pad = jnp.concatenate([zero_plane, interior, zero_plane], axis=-1)
    numerator = (
        source
        + k_west * padded[..., :-2, 1:-1, :]
        + k_east * padded[..., 2:, 1:-1, :]
        + k_south * padded[..., 1:-1, :-2, :]
        + k_north * padded[..., 1:-1, 2:, :]
        + k_below * column_pad[..., :-2]
        + k_above * column_pad[..., 2:]
    )
    return numerator * inverse


def share_multipliers(own_multiplier):
    return extended(own_multiplier[None, None], (("gx", 0), ("gy", 1)), 1)


def on_device(
    velocity, forcing, viscosity, multipliers, sphere_centres, sphere_offsets, sphere_count
):
    width_x = velocity.shape[1]
    width_y = velocity.shape[2]
    height = velocity.shape[3]
    slots = multipliers.shape[2]
    points = multipliers.shape[4]
    cell_count = width_x * width_y * height
    live_slot = jnp.arange(slots) < sphere_count[0, 0]
    centres = sphere_centres[0, 0]
    offsets = sphere_offsets[0, 0]
    parked = jnp.where(live_slot, 0, -8 * width_x).astype(jnp.int32)
    owned_x = centres[:, 0:1] + offsets[:, 0, :] + parked[:, None]
    owned_y = centres[:, 1:2] + offsets[:, 1, :]
    owned_z = centres[:, 2:3] + offsets[:, 2, :]
    geometry = jnp.concatenate([jnp.stack([owned_x, owned_y, owned_z], 1), offsets], 1)
    nearby = extended(geometry[None, None], (("gx", 0), ("gy", 1)), 1)
    shift_x = ((jnp.arange(3) - 1) * width_x)[:, None, None, None]
    shift_y = ((jnp.arange(3) - 1) * width_y)[None, :, None, None]
    local_x = nearby[:, :, :, 0, :] + shift_x
    local_y = nearby[:, :, :, 1, :] + shift_y
    local_z = nearby[:, :, :, 2, :]
    inside = (local_x >= 0) & (local_x < width_x) & (local_y >= 0) & (local_y < width_y)
    flat_cells = jnp.where(inside, (local_x * width_y + local_y) * height + local_z, 0).reshape(-1)
    marker_mask = inside.astype(jnp.float32)[:, :, :, None, :]
    own_radius = offsets.astype(jnp.float32)
    spread_sum = jnp.sum(own_radius * own_radius, axis=(1, 2))
    viscous_rim = extended(viscosity, (("gx", 0), ("gy", 1)), 1)
    full_terms = face_terms(viscous_rim)

    def relax_flow(flow, source):
        for sweep_index in range(SWEEPS):
            padded = extended(flow, (("gx", 1), ("gy", 2)), 1)
            flow = jacobi_step(padded, full_terms, source)
        return flow

    flow = velocity
    mean_velocity = None
    spin = None
    own_multiplier = multipliers[0, 0]
    for round_index in range(UZ):
        near_multiplier = share_multipliers(own_multiplier)
        weighted = jnp.moveaxis(near_multiplier * marker_mask, 3, 0).reshape(3, -1)
        summed = jnp.zeros((3, cell_count), jnp.float32).at[:, flat_cells].add(weighted)
        flow = relax_flow(flow, forcing + summed.reshape(velocity.shape))
        picked = flow.reshape(3, -1)[:, flat_cells].reshape((3, 3, 3, slots, points))
        returned = extended(jnp.moveaxis(picked, 0, 3) * marker_mask, (("gx", 0), ("gy", 1)), 1)
        own_sampled = jnp.sum(returned[0::2, 0::2], axis=(0, 1))
        mean_velocity = jnp.sum(own_sampled, -1) / points
        spin = 1.5 * jnp.sum(cross_product(own_radius, own_sampled), -1) / spread_sum[:, None]
        if round_index + 1 < UZ:
            target = mean_velocity[..., None] + cross_product(spin[..., None], own_radius)
            own_multiplier = own_multiplier + UZAWA_STEP * (target - own_sampled)
    motion = jnp.concatenate([mean_velocity, spin], -1)
    return (flow, motion[None, None])


def solution(mesh):
    placed = (
        P(None, "gx", "gy", None),
        P(None, "gx", "gy", None),
        P("gx", "gy", None),
        P("gx", "gy", None, None, None),
        P("gx", "gy", None, None),
        P("gx", "gy", None, None, None),
        P("gx", "gy"),
    )
    return jax.shard_map(
        on_device,
        mesh=mesh,
        in_specs=placed,
        out_specs=(P(None, "gx", "gy", None), P("gx", "gy", None, None)),
        check_vma=False,
    )
```

profile of v0, /device:TPU:0, one launch (start us, length us, event | category | flops | bytes accessed | tf_op | source)
XLA Modules:
  0.0 1197.1 jit_solution(12814486538027742040)
XLA Ops:
  33.6 6.2 collective-permute-done.2
  39.8 4.1 collective-permute-start.15
  45.2 7.6 copy.420
  52.8 191.8 %scatter_custom_fusion = f32[3,32768]{0,1:T(8,128)} fusion(s32[27648]{0:T(1024)S(1)} %bitcast.141, f32[27648,3]{1,0:T(8,128)} %copy.420, f32[]{:T(128)} %constant.14.clone.1), kind=kCustom, calls=%fused_computation.10 | custom fusion | flops 82944 | bytes 393728 | tf_op jit(solution)/shard_map/scatter-add | solution.py:118
  244.6 10.0 copy.421
  270.4 3.9 collective-permute-start.23
  287.0 8.7 copy.422
  295.8 97.3 %gather_fusion = f32[27648,3]{1,0:T(8,128)} fusion(f32[3,32768]{0,1:T(8,128)} %bitcast.126, s32[27648]{0:T(1024)S(1)} %broadcast_clamp_fusion), kind=kCustom, calls=%fused_computation | custom fusion | bytes 774144 | tf_op jit(solution)/shard_map/gather | solution.py:120
  393.0 9.6 copy.423
  412.5 5.5 collective-permute-done.30
  433.6 7.6 copy.430
  441.2 191.8 %scatter_custom_fusion.1 = f32[3,32768]{0,1:T(8,128)} fusion(s32[27648]{0:T(1024)S(1)} %bitcast.143, f32[27648,3]{1,0:T(8,128)} %copy.430, f32[]{:T(128)} %constant.14.clone.1), kind=kCustom, calls=%fused_computation.8 | custom fusion | flops 82944 | bytes 393728 | tf_op jit(solution)/shard_map/scatter-add | solution.py:118
  633.0 10.0 copy.431
  675.2 8.7 copy.432
  683.9 97.3 %gather_fusion.1 = f32[27648,3]{1,0:T(8,128)} fusion(f32[3,32768]{0,1:T(8,128)} %bitcast.127, s32[27648]{0:T(1024)S(1)} %broadcast_clamp_fusion), kind=kCustom, calls=%fused_computation.1 | custom fusion | bytes 774144 | tf_op jit(solution)/shard_map/gather | solution.py:120
  781.2 9.6 copy.433
  800.6 5.4 collective-permute-done.54
  821.8 7.6 copy.440
  829.4 191.8 %scatter_custom_fusion.2 = f32[3,32768]{0,1:T(8,128)} fusion(s32[27648]{0:T(1024)S(1)} %bitcast.144, f32[27648,3]{1,0:T(8,128)} %copy.440, f32[]{:T(128)} %constant.14.clone.1), kind=kCustom, calls=%fused_computation.6 | custom fusion | flops 82944 | bytes 393728 | tf_op jit(solution)/shard_map/scatter-add | solution.py:118
  1021.3 10.0 copy.441
  1063.5 8.7 copy.442
  1072.2 97.3 %gather_fusion.2 = f32[27648,3]{1,0:T(8,128)} fusion(f32[3,32768]{0,1:T(8,128)} %bitcast.125, s32[27648]{0:T(1024)S(1)} %broadcast_clamp_fusion), kind=kCustom, calls=%fused_computation.2 | custom fusion | bytes 774144 | tf_op jit(solution)/shard_map/gather | solution.py:120
  1169.5 9.6 copy.443
  1188.9 5.5 collective-permute-done.78
  (280 shorter events, 189.4 us)
Async XLA Ops:
  3.6 26.0 %collective-permute-start = (s32[1,1,8,6,384]{4,2,3,1,0:T(8,128)S(1)}, s32[1,1,8,6,384]{4,2,3,1,0:T(8,128)S(1)}, u32[]{:S(2)}, u32[]{:S(2)}) collective-permute-start(s32[1,1,8,6,384]{4,2,3,1,0:T(8,128)S(1)} %add_bitcast_fusion), channel_id=1, source_target_pairs={{0,4},{4,8},{8,12},{12,16},{16,20},{20,24},{24,28},{28,0},{1,5},{5... | collective-permute-start | bytes 221192 | tf_op jit(solution)/shard_map/ppermute | solution.py:21
  4.0 25.5 %collective-permute-start.1 = (s32[1,1,8,6,384]{4,2,3,1,0:T(8,128)S(1)}, s32[1,1,8,6,384]{4,2,3,1,0:T(8,128)S(1)}, u32[]{:S(2)}, u32[]{:S(2)}) collective-permute-start(s32[1,1,8,6,384]{4,2,3,1,0:T(8,128)S(1)} %add_bitcast_fusion), channel_id=1, source_target_pairs={{4,0},{8,4},{12,8},{16,12},{20,16},{24,20},{28,24},{0,28},{5,1},{9... | collective-permute-start | bytes 221192 | tf_op jit(solution)/shard_map/ppermute | solution.py:24
  7.0 14.2 %collective-permute-start.4 = (f32[1,1,8,3,384]{4,2,3,1,0:T(8,128)}, f32[1,1,8,3,384]{4,2,3,1,0:T(8,128)S(1)}, u32[]{:S(2)}, u32[]{:S(2)}) collective-permute-start(f32[1,1,8,3,384]{4,2,3,1,0:T(8,128)} %param.10), channel_id=1, source_target_pairs={{0,4},{4,8},{8,12},{12,16},{16,20},{20,24},{24,28},{28,0},{1,5},{5... | collective-permute-start | bytes 110600 | tf_op jit(solution)/shard_map/ppermute | solution.py:21
  21.1 8.4 collective-permute-start.11
  24.6 20.3 %collective-permute-start.6 = (f32[3,1,8,3,384]{4,2,3,1,0:T(8,128)S(1)}, f32[3,1,8,3,384]{4,2,3,1,0:T(8,128)S(1)}, u32[]{:S(2)}, u32[]{:S(2)}) collective-permute-start(f32[3,1,8,3,384]{4,2,3,1,0:T(8,128)S(1)} %constant_dynamic-update-slice_fusion), channel_id=1, source_target_pairs={{0,1},{1,2},{2,3},{3,0},{4,5},{5,6},{6,7},{7,4},{8,9},{9,10},{10,1... | collective-permute-start | bytes 331784 | tf_op jit(solution)/shard_map/ppermute | solution.py:21
  25.2 19.7 %collective-permute-start.7 = (f32[3,1,8,3,384]{4,2,3,1,0:T(8,128)S(1)}, f32[3,1,8,3,384]{4,2,3,1,0:T(8,128)S(1)}, u32[]{:S(2)}, u32[]{:S(2)}) collective-permute-start(f32[3,1,8,3,384]{4,2,3,1,0:T(8,128)S(1)} %constant_dynamic-update-slice_fusion), channel_id=1, source_target_pairs={{1,0},{2,1},{3,2},{0,3},{5,4},{6,5},{7,6},{4,7},{9,8},{10,9},{11,1... | collective-permute-start | bytes 331784 | tf_op jit(solution)/shard_map/ppermute | solution.py:24
  29.6 10.2 collective-permute-start.2
  29.7 14.3 %collective-permute-start.3 = (s32[3,1,8,6,384]{4,2,3,1,0:T(8,128)S(1)}, s32[3,1,8,6,384]{4,2,3,1,0:T(8,128)S(1)}, u32[]{:S(2)}, u32[]{:S(2)}) collective-permute-start(s32[3,1,8,6,384]{4,2,3,1,0:T(8,128)S(1)} %pad_add_fusion), channel_id=1, source_target_pairs={{1,0},{2,1},{3,2},{0,3},{5,4},{6,5},{7,6},{4,7},{9,8},{10,9},{11,1... | collective-permute-start | bytes 663560 | tf_op jit(solution)/shard_map/ppermute | solution.py:24
  33.5 221.1 %collective-permute-start.13 = (f32[3,10,1,128]{3,2,1,0:T(1,128)S(1)}, f32[3,10,1,128]{3,2,1,0:T(1,128)S(1)}, u32[]{:S(2)}, u32[]{:S(2)}) collective-permute-start(f32[3,10,1,128]{3,2,1,0:T(1,128)S(1)} %get-tuple-element.76), channel_id=1, source_target_pairs={{0,1},{1,2},{2,3},{3,0},{4,5},{5,6},{6,7},{7,4},{8,9},{9,10},{10,1... | collective-permute-start | bytes 46088 | tf_op jit(solution)/shard_map/ppermute | solution.py:21
  39.8 214.8 %collective-permute-start.15 = (f32[3,10,1,128]{3,2,1,0:T(1,128)S(1)}, f32[3,10,1,128]{3,2,1,0:T(1,128)S(1)}, u32[]{:S(2)}, u32[]{:S(2)}) collective-permute-start(f32[3,10,1,128]{3,2,1,0:T(1,128)S(1)} %get-tuple-element.77), channel_id=1, source_target_pairs={{1,0},{2,1},{3,2},{0,3},{5,4},{6,5},{7,6},{4,7},{9,8},{10,9},{11,1... | collective-permute-start | bytes 46088 | tf_op jit(solution)/shard_map/ppermute | solution.py:24
  408.6 9.4 collective-permute-start.30
  409.4 10.1 collective-permute-start.31
  422.7 6.6 collective-permute-start.36
  425.4 7.8 collective-permute-start.34
  429.4 213.6 %collective-permute-start.38 = (f32[3,10,1,128]{3,2,1,0:T(1,128)S(1)}, f32[3,10,1,128]{3,2,1,0:T(1,128)S(1)}, u32[]{:S(2)}, u32[]{:S(2)}) collective-permute-start(f32[3,10,1,128]{3,2,1,0:T(1,128)S(1)} %get-tuple-element.68), channel_id=1, source_target_pairs={{0,1},{1,2},{2,3},{3,0},{4,5},{5,6},{6,7},{7,4},{8,9},{9,10},{10,1... | collective-permute-start | bytes 46088 | tf_op jit(solution)/shard_map/ppermute | solution.py:21
  429.8 213.2 %collective-permute-start.39 = (f32[3,10,1,128]{3,2,1,0:T(1,128)S(1)}, f32[3,10,1,128]{3,2,1,0:T(1,128)S(1)}, u32[]{:S(2)}, u32[]{:S(2)}) collective-permute-start(f32[3,10,1,128]{3,2,1,0:T(1,128)S(1)} %get-tuple-element.69), channel_id=1, source_target_pairs={{1,0},{2,1},{3,2},{0,3},{5,4},{6,5},{7,6},{4,7},{9,8},{10,9},{11,1... | collective-permute-start | bytes 46088 | tf_op jit(solution)/shard_map/ppermute | solution.py:24
  796.7 9.4 collective-permute-start.54
  797.6 10.2 collective-permute-start.55
  811.0 6.6 collective-permute-start.60
  813.7 7.8 collective-permute-start.58
  817.6 213.6 %collective-permute-start.62 = (f32[3,10,1,128]{3,2,1,0:T(1,128)S(1)}, f32[3,10,1,128]{3,2,1,0:T(1,128)S(1)}, u32[]{:S(2)}, u32[]{:S(2)}) collective-permute-start(f32[3,10,1,128]{3,2,1,0:T(1,128)S(1)} %get-tuple-element.60), channel_id=1, source_target_pairs={{0,1},{1,2},{2,3},{3,0},{4,5},{5,6},{6,7},{7,4},{8,9},{9,10},{10,1... | collective-permute-start | bytes 46088 | tf_op jit(solution)/shard_map/ppermute | solution.py:21
  817.8 213.5 %collective-permute-start.63 = (f32[3,10,1,128]{3,2,1,0:T(1,128)S(1)}, f32[3,10,1,128]{3,2,1,0:T(1,128)S(1)}, u32[]{:S(2)}, u32[]{:S(2)}) collective-permute-start(f32[3,10,1,128]{3,2,1,0:T(1,128)S(1)} %get-tuple-element.61), channel_id=1, source_target_pairs={{1,0},{2,1},{3,2},{0,3},{5,4},{6,5},{7,6},{4,7},{9,8},{10,9},{11,1... | collective-permute-start | bytes 46088 | tf_op jit(solution)/shard_map/ppermute | solution.py:24
  1185.0 9.4 collective-permute-start.78
  1185.9 10.3 collective-permute-start.79
  (61 other events, 1059.1 us)
where the time goes:
time: 1200 us
  other arithmetic  585 us (49%)
  local copies, waits for them, and re-layouts  406 us (34%)
  starting transfers between devices  131 us (11%)
  waiting for transfers between devices  72.6 us (6%)
    scatter-add x3, other arithmetic, on_device(): jnp.zeros((3, cell_count), jnp.float32).at[:, flat_cells].add(weighted)  576 us
    gather x3, local copies, waits for them, and re-layouts, on_device(): flow.reshape(3, -1)[:, flat_cells].reshape((3, 3, 3, slots, points))  292 us
    ppermute x40, starting transfers between devices, extended(): lax.ppermute(lax.slice_in_dim(block, 0, width, axis=dim), axis, backward)  112 us
    ppermute x40, waiting for transfers between devices, extended(): lax.ppermute(lax.slice_in_dim(block, block.shape[dim] - width, None, axis...  67 us
    reshape x3, local copies, waits for them, and re-layouts, on_device(): flow = relax_flow(flow, forcing + summed.reshape(velocity.shape))  29.9 us
    reshape x3, local copies, waits for them, and re-layouts, on_device(): flow.reshape(3, -1)[:, flat_cells].reshape((3, 3, 3, slots, points))  28.7 us
    mul x3, local copies, waits for them, and re-layouts, jacobi_step(): return numerator * inverse  26.2 us
  transfers between devices with their start and end apart: 80, of which 32 were waited for; matrix products, arithmetic and copies ran while one was open for 53% of the time, Pallas kernels for 0%

commit v1 on v0

v1 whole, which is shorter than its diff:
```python
import functools

import jax
import jax.numpy as jnp
from jax import lax
from jax.experimental import pallas as pl
from jax.experimental.pallas import tpu as pltpu
from jax.sharding import PartitionSpec as P

SWEEPS = 4
UZ = 3
REACH = 8
WINDOW = 24

MASS_TERM = 0.2
VERTICAL_WEIGHT = 0.25
UZAWA_STEP = 0.5

MESH = pl.DeviceIdType.MESH
VM = pl.BlockSpec(memory_space=pltpu.VMEM)
SM = pl.BlockSpec(memory_space=pltpu.SMEM)
F32 = jnp.float32
BF16 = jnp.bfloat16


def around():
    nx, ny = lax.axis_size("gx"), lax.axis_size("gy")
    me_x, me_y = lax.axis_index("gx"), lax.axis_index("gy")
    left = (lax.rem(me_x + nx - 1, nx), me_y)
    right = (lax.rem(me_x + 1, nx), me_y)
    down = (me_x, lax.rem(me_y + ny - 1, ny))
    up = (me_x, lax.rem(me_y + 1, ny))
    return left, right, down, up


def greet(devices):
    barrier = pltpu.get_barrier_semaphore()
    for device in devices:
        pl.semaphore_signal(barrier, inc=1, device_id=device, device_id_type=MESH)
    pl.semaphore_wait(barrier, len(devices))


def send(src, dst, sems, index, device):
    copy = pltpu.make_async_remote_copy(
        src_ref=src,
        dst_ref=dst,
        send_sem=sems.at[0, index],
        recv_sem=sems.at[1, index],
        device_id=device,
        device_id_type=MESH,
    )
    copy.start()
    return copy


def scatter_kernel(meta, key, depth, lam, out):
    width_x = out.shape[1]
    height = out.shape[3]
    rows = width_x * WINDOW
    slots, points = key.shape
    out[...] = jnp.zeros_like(out)

    def one(s, carry):
        @pl.when(meta[1, s] > 0)
        def _():
            base = pl.multiple_of(meta[0, s], 8)
            row_key = key[pl.ds(s, 1), :]
            row_z = depth[pl.ds(s, 1), :]
            mask = lax.broadcasted_iota(jnp.int32, (rows, points), 0) == row_key
            mask = jnp.where(mask, 1.0, 0.0).astype(BF16)
            at_z = lax.broadcasted_iota(jnp.int32, (height, points), 0) == row_z
            high, low = [], []
            for c in range(3):
                value = lam[c, pl.ds(s, 1), :]
                top = value.astype(BF16).astype(F32)
                high.append(jnp.where(at_z, top, 0.0).astype(BF16))
                low.append(jnp.where(at_z, value - top, 0.0).astype(BF16))
            dims = (((1,), (1,)), ((), ()))
            got = lax.dot_general(
                mask, jnp.concatenate(high, 0), dims, preferred_element_type=F32
            ) + lax.dot_general(
                mask, jnp.concatenate(low, 0), dims, preferred_element_type=F32
            )
            for c in range(3):
                part = got[:, c * height:(c + 1) * height].reshape(width_x, WINDOW, height)
                out[c, :, pl.ds(base, WINDOW), :] += part

        return carry

    lax.fori_loop(0, slots, one, 0)


def gather_kernel(meta, key, depth, field, out):
    width_x = field.shape[1]
    height = field.shape[3]
    rows = width_x * WINDOW
    slots, points = key.shape
    out[...] = jnp.zeros_like(out)

    def one(s, carry):
        @pl.when(meta[1, s] > 0)
        def _():
            base = pl.multiple_of(meta[0, s], 8)
            row_key = key[pl.ds(s, 1), :]
            row_z = depth[pl.ds(s, 1), :]
            mask = lax.broadcasted_iota(jnp.int32, (rows, points), 0) == row_key
            at_z = lax.broadcasted_iota(jnp.int32, (height, points), 0) == row_z
            at_z = jnp.where(at_z, 1.0, 0.0).astype(BF16)
            at_z = jnp.concatenate([at_z, at_z], 0)
            for c in range(3):
                value = field[c, :, pl.ds(base, WINDOW), :].reshape(rows, height)
                top = value.astype(BF16)
                rest = (value - top.astype(F32)).astype(BF16)
                got = jnp.dot(
                    jnp.concatenate([top, rest], 1), at_z, preferred_element_type=F32
                )
                out[c, pl.ds(s, 1), :] = jnp.sum(
                    jnp.where(mask, got, 0.0), axis=0, keepdims=True
                )

        return carry

    lax.fori_loop(0, slots, one, 0)


def relax_kernel(
    flow, forcing, partial, terms, out, work, source, xh, ys, yh, ph, gh, xsem, ysem, psem, gsem
):
    left, right, down, up = around()
    width_x, width_y, height = flow.shape[1:]
    lo, hi = REACH, REACH + width_y
    greet((left, right, down, up))
    share = [
        send(partial.at[:, :, pl.ds(0, REACH), :], ph.at[1], psem, 1, down),
        send(partial.at[:, :, pl.ds(hi, REACH), :], ph.at[0], psem, 0, up),
    ]
    sends = []

    def exchange(step, x_ref, first_row, last_row):
        for c in range(3):
            ys[step, 1, c] = x_ref[c, :, first_row, :]
            ys[step, 0, c] = x_ref[c, :, last_row, :]
        rows = pl.ds(first_row, width_y)
        return [
            send(x_ref.at[:, 0, rows, :], xh.at[step, 1], xsem.at[step], 1, left),
            send(x_ref.at[:, width_x - 1, rows, :], xh.at[step, 0], xsem.at[step], 0, right),
            send(ys.at[step, 1], yh.at[step, 1], ysem.at[step], 1, down),
            send(ys.at[step, 0], yh.at[step, 0], ysem.at[step], 0, up),
        ]

    sends = exchange(0, flow, 0, width_y - 1)
    work[0, :, :, lo:hi, :] = flow[...]
    for copy in share:
        copy.wait()
    source[...] = forcing[...] + partial[:, :, lo:hi, :]
    source[:, :, 0:REACH, :] += ph[0]
    source[:, :, width_y - REACH:width_y, :] += ph[1]
    source[...] = source[...] * terms[6][None]

    for step in range(SWEEPS):
        for copy in sends:
            copy.wait()
        for c in range(3):
            for i in range(width_x):
                work[step, c, i, lo - 1:lo, :] = yh[step, 0, c, i:i + 1, :]
                work[step, c, i, hi:hi + 1, :] = yh[step, 1, c, i:i + 1, :]
        target = work.at[step + 1] if step + 1 < SWEEPS else out

        def component(c, carry):
            for i in range(width_x):
                here = work[step, c, i, lo:hi, :]
                west = xh[step, 0, c] if i == 0 else work[step, c, i - 1, lo:hi, :]
                east = xh[step, 1, c] if i == width_x - 1 else work[step, c, i + 1, lo:hi, :]
                south = work[step, c, i, lo - 1:hi - 1, :]
                north = work[step, c, i, lo + 1:hi + 1, :]
                target[c, i, lo:hi, :] = (
                    source[c, i]
                    + terms[0, i] * west
                    + terms[1, i] * east
                    + terms[2, i] * south
                    + terms[3, i] * north
                    + terms[4, i] * pltpu.roll(here, 1, 1)
                    + terms[5, i] * pltpu.roll(here, height - 1, 1)
                )
            return carry

        lax.fori_loop(0, 3, component, 0)
        if step + 1 < SWEEPS:
            sends = exchange(step + 1, target, lo, hi - 1)

    last = [
        send(out.at[:, :, pl.ds(lo, REACH), :], gh.at[1], gsem, 1, down),
        send(out.at[:, :, pl.ds(hi - REACH, REACH), :], gh.at[0], gsem, 0, up),
    ]
    for copy in last:
        copy.wait()
    out[:, :, 0:lo, :] = gh[0]
    out[:, :, hi:hi + REACH, :] = gh[1]


def body_kernel(final, sampled, radius, lam, out, motion, wh, lh, new, wsem, lsem):
    left, right, _, _ = around()
    slots, points = radius.shape[1:]
    greet((left, right))
    sends = [
        send(sampled.at[:, pl.ds(0, slots), :], wh.at[1], wsem, 1, left),
        send(sampled.at[:, pl.ds(2 * slots, slots), :], wh.at[0], wsem, 0, right),
    ]
    r = [radius[c] for c in range(3)]
    spread = jnp.sum(r[0] * r[0] + r[1] * r[1] + r[2] * r[2], axis=1, keepdims=True)
    for copy in sends:
        copy.wait()
    w = [sampled[c, slots:2 * slots, :] + wh[0, c] + wh[1, c] for c in range(3)]
    mean = [jnp.sum(w[c], axis=1, keepdims=True) / points for c in range(3)]
    spin = []
    for c in range(3):
        a, b = (c + 1) % 3, (c + 2) % 3
        moment = jnp.sum(r[a] * w[b] - r[b] * w[a], axis=1, keepdims=True)
        spin.append(1.5 * moment / spread)
    lane = lax.broadcasted_iota(jnp.int32, motion.shape, 1)
    row = jnp.zeros(motion.shape, F32)
    for c, value in enumerate(mean + spin):
        row = jnp.where(lane == c, value, row)
    motion[...] = row
    if final:
        out[...] = jnp.zeros_like(out)
        return
    for c in range(3):
        a, b = (c + 1) % 3, (c + 2) % 3
        target = mean[c] + (spin[a] * r[b] - spin[b] * r[a])
        new[c] = lam[c, slots:2 * slots, :] + UZAWA_STEP * (target - w[c])
    sends = [
        send(new, lh.at[1], lsem, 1, left),
        send(new, lh.at[0], lsem, 0, right),
    ]
    out[:, slots:2 * slots, :] = new[...]
    for copy in sends:
        copy.wait()
    out[:, 0:slots, :] = lh[0]
    out[:, 2 * slots:3 * slots, :] = lh[1]


def pair(block, axis, dim, width):
    count = lax.axis_size(axis)
    forward = [(i, (i + 1) % count) for i in range(count)]
    backward = [(target, source) for source, target in forward]
    size = block.shape[dim]
    low = lax.ppermute(lax.slice_in_dim(block, size - width, size, axis=dim), axis, forward)
    high = lax.ppermute(lax.slice_in_dim(block, 0, width, axis=dim), axis, backward)
    return jnp.concatenate([low, block, high], axis=dim)


def face_terms(nu):
    along_x = pair(nu, "gx", 0, 1)
    along_y = pair(nu, "gy", 1, 1)
    along_z = jnp.concatenate([nu[:, :, :1], nu, nu[:, :, -1:]], axis=2)
    k = [
        0.5 * (nu + along_x[:-2]),
        0.5 * (nu + along_x[2:]),
        0.5 * (nu + along_y[:, :-2]),
        0.5 * (nu + along_y[:, 2:]),
        VERTICAL_WEIGHT * 0.5 * (nu + along_z[:, :, :-2]),
        VERTICAL_WEIGHT * 0.5 * (nu + along_z[:, :, 2:]),
    ]
    inverse = 1.0 / (MASS_TERM + k[0] + k[1] + k[2] + k[3] + k[4] + k[5])
    z = jnp.arange(nu.shape[2])
    k[4] = jnp.where(z == 0, 0.0, k[4])
    k[5] = jnp.where(z == nu.shape[2] - 1, 0.0, k[5])
    return jnp.stack([face * inverse for face in k] + [inverse])


def on_device(
    velocity, forcing, viscosity, multipliers, sphere_centres, sphere_offsets, sphere_count
):
    _, width_x, width_y, height = velocity.shape
    slots, points = multipliers.shape[2], multipliers.shape[4]
    live = jnp.arange(slots) < sphere_count[0, 0]
    centres = sphere_centres[0, 0]
    offsets = jnp.moveaxis(sphere_offsets[0, 0], 1, 0)
    base = (centres[:, 1] // 8) * 8
    own_x = jnp.where(live[:, None], centres[:, 0:1] + offsets[0], -8 * width_x)
    own_y = (centres[:, 1] - base)[:, None] + offsets[1] + REACH
    own_z = centres[:, 2:3] + offsets[2]
    geometry = jnp.stack(
        [own_x, own_y, own_z, jnp.broadcast_to(base[:, None], own_x.shape)]
    ).astype(jnp.int32)
    near = pair(geometry, "gx", 1, slots)
    shift = jnp.repeat((jnp.arange(3) - 1) * width_x, slots)[:, None]
    local_x = near[0] + shift
    inside = (local_x >= 0) & (local_x < width_x)
    key = jnp.where(inside, local_x * WINDOW + near[1], -1).astype(jnp.int32)
    depth = near[2]
    meta = jnp.stack([near[3, :, 0], jnp.any(inside, 1).astype(jnp.int32)])
    radius = offsets.astype(F32)
    lam = pair(jnp.moveaxis(multipliers[0, 0], 1, 0), "gx", 1, slots)
    terms = face_terms(viscosity)

    wide = (3, width_x, width_y + 2 * REACH, height)
    shape = jax.ShapeDtypeStruct
    limit = 48 * 1024 * 1024
    scatter = pl.pallas_call(
        scatter_kernel,
        name="spread_force",
        out_shape=shape(wide, F32),
        in_specs=[SM, VM, VM, VM],
        out_specs=VM,
        compiler_params=pltpu.CompilerParams(vmem_limit_bytes=limit),
    )
    gather = pl.pallas_call(
        gather_kernel,
        name="sample_flow",
        out_shape=shape((3, 3 * slots, points), F32),
        in_specs=[SM, VM, VM, VM],
        out_specs=VM,
        compiler_params=pltpu.CompilerParams(vmem_limit_bytes=limit),
    )
    relax = pl.pallas_call(
        relax_kernel,
        name="relax_flow",
        out_shape=shape(wide, F32),
        in_specs=[VM] * 4,
        out_specs=VM,
        scratch_shapes=[
            pltpu.VMEM((SWEEPS,) + wide, F32),
            pltpu.VMEM((3, width_x, width_y, height), F32),
            pltpu.VMEM((SWEEPS, 2, 3, width_y, height), F32),
            pltpu.VMEM((SWEEPS, 2, 3, width_x, height), F32),
            pltpu.VMEM((SWEEPS, 2, 3, width_x, height), F32),
            pltpu.VMEM((2, 3, width_x, REACH, height), F32),
            pltpu.VMEM((2, 3, width_x, REACH, height), F32),
            pltpu.SemaphoreType.DMA((SWEEPS, 2, 2)),
            pltpu.SemaphoreType.DMA((SWEEPS, 2, 2)),
            pltpu.SemaphoreType.DMA((2, 2)),
            pltpu.SemaphoreType.DMA((2, 2)),
        ],
        compiler_params=pltpu.CompilerParams(
            collective_id=1, has_side_effects=True, vmem_limit_bytes=limit
        ),
    )

    def body(final):
        return pl.pallas_call(
            functools.partial(body_kernel, final),
            name="fit_last" if final else "fit_body",
            out_shape=(shape((3, 3 * slots, points), F32), shape((slots, 128), F32)),
            in_specs=[VM] * 3,
            out_specs=(VM, VM),
            scratch_shapes=[
                pltpu.VMEM((2, 3, slots, points), F32),
                pltpu.VMEM((2, 3, slots, points), F32),
                pltpu.VMEM((3, slots, points), F32),
                pltpu.SemaphoreType.DMA((2, 2)),
                pltpu.SemaphoreType.DMA((2, 2)),
            ],
            compiler_params=pltpu.CompilerParams(
                collective_id=3 if final else 2, has_side_effects=True, vmem_limit_bytes=limit
            ),
        )

    flow = velocity
    motion = None
    for round_index in range(UZ):
        force = scatter(meta, key, depth, lam)
        field = relax(flow, forcing, force, terms)
        flow = field[:, :, REACH:REACH + width_y, :]
        sampled = gather(meta, key, depth, field)
        lam, motion = body(round_index + 1 == UZ)(sampled, radius, lam)
    return flow, motion[:, :6][None, None]


def solution(mesh):
    placed = (
        P(None, "gx", "gy", None),
        P(None, "gx", "gy", None),
        P("gx", "gy", None),
        P("gx", "gy", None, None, None),
        P("gx", "gy", None, None),
        P("gx", "gy", None, None, None),
        P("gx", "gy"),
    )
    return jax.shard_map(
        on_device,
        mesh=mesh,
        in_specs=placed,
        out_specs=(P(None, "gx", "gy", None), P("gx", "gy", None, None)),
        check_vma=False,
    )
```

time: 1200 us -> 154 us (0.13)
  other arithmetic: 585 us -> 1.03 us
  local copies, waits for them, and re-layouts: 406 us -> 3.41 us
  Pallas kernels: 0 us -> 134 us
  starting transfers between devices: 131 us -> 12.1 us
  waiting for transfers between devices: 72.6 us -> 1.58 us
    scatter-add x3 -> x0, other arithmetic: 576 us -> none  [on_device(): jnp.zeros((3, cell_count), jnp.float32).at[:, flat_cells].add(weighted)]
    gather x3 -> x0, local copies, waits for them, and re-layouts: 292 us -> none  [on_device(): flow.reshape(3, -1)[:, flat_cells].reshape((3, 3, 3, slots, points))]
    pallas_call x0 -> x12, Pallas kernels: none -> 134 us  [the longest x3 92.4 us: on_device(): field = relax(flow, forcing, force, terms)]
    ppermute x80 -> x8, starting transfers between devices: 131 us -> 12.1 us  [the longest x4 10.5 us: pair(): lax.ppermute(lax.slice_in_dim(block, 0, width, axis=dim), axis, backward)]
    reshape x9 -> x0, local copies, waits for them, and re-layouts: 81.4 us -> none  [the longest x3 29.9 us: on_device(): flow = relax_flow(flow, forcing + summed.reshape(velocity.shape))]
    ppermute x80 -> x8, waiting for transfers between devices: 72.6 us -> 1.58 us  [the longest x4 1.57 us: pair(): lax.ppermute(lax.slice_in_dim(block, size - width, size, axis=dim), axis,...]
    mul x5 -> x0, local copies, waits for them, and re-layouts: 26.2 us -> none  [the longest x3 26.2 us: jacobi_step(): return numerator * inverse]
  transfers between devices with their start and end apart: 80 -> 8, of which waited for: 32 -> 2; matrix products, arithmetic and copies ran while one was open for 53% -> 1% of each run, Pallas kernels for 0% -> 0%
where the time goes in v1:
time: 154 us
  Pallas kernels  134 us (87%)
  starting transfers between devices  12.1 us (8%)
  local copies, waits for them, and re-layouts  3.41 us (2%)
  between operations  1.61 us (1%)
  waiting for transfers between devices  1.58 us (1%)
    pallas_call x3, Pallas kernels, on_device(): field = relax(flow, forcing, force, terms)  92.4 us
    pallas_call x3, Pallas kernels, on_device(): lam, motion = body(round_index + 1 == UZ)(sampled, radius, lam)  20.9 us
    pallas_call x3, Pallas kernels, on_device(): force = scatter(meta, key, depth, lam)  11 us
    ppermute x4, starting transfers between devices, pair(): lax.ppermute(lax.slice_in_dim(block, 0, width, axis=dim), axis, backward)  10.5 us
    pallas_call x3, Pallas kernels, on_device(): sampled = gather(meta, key, depth, field)  9.45 us
  transfers between devices with their start and end apart: 8, of which 2 were waited for; matrix products, arithmetic and copies ran while one was open for 1% of the time, Pallas kernels for 0%

profile of v1, /device:TPU:0, one launch (start us, length us, event | category | flops | bytes accessed | tf_op | source)
XLA Modules:
  0.0 153.5 jit_solution(12163390862121527445)
XLA Ops:
  0.6 0.8 fusion.19
  1.4 3.3 %collective-permute-start.5 = (f32[1,32,128]{2,1,0:T(8,128)S(1)}, f32[1,32,128]{2,1,0:T(8,128)S(1)}, u32[]{:S(2)}, u32[]{:S(2)}) collective-permute-start(f32[1,32,128]{2,1,0:T(8,128)S(1)} %get-tuple-element.16), channel_id=1, source_target_pairs={{4,0},{8,4},{12,8},{16,12},{20,16},{24,20},{28,24},{0,28},{5,1},{9... | collective-permute-start | bytes 49160 | tf_op jit(solution)/shard_map/ppermute | solution.py:249
  4.7 0.8 fusion.20
  5.5 1.6 %collective-permute-start.6 = (f32[8,1,128]{2,1,0:T(1,128)S(1)}, f32[8,1,128]{2,1,0:T(1,128)S(1)}, u32[]{:S(2)}, u32[]{:S(2)}) collective-permute-start(f32[8,1,128]{2,1,0:T(1,128)S(1)} %get-tuple-element.18), channel_id=1, source_target_pairs={{0,1},{1,2},{2,3},{3,0},{4,5},{5,6},{6,7},{7,4},{8,9},{9,10},{10,1... | collective-permute-start | bytes 12296 | tf_op jit(solution)/shard_map/ppermute | solution.py:248
  7.1 2.2 %collective-permute-start.7 = (f32[8,1,128]{2,1,0:T(1,128)S(1)}, f32[8,1,128]{2,1,0:T(1,128)S(1)}, u32[]{:S(2)}, u32[]{:S(2)}) collective-permute-start(f32[8,1,128]{2,1,0:T(1,128)S(1)} %get-tuple-element.19), channel_id=1, source_target_pairs={{1,0},{2,1},{3,2},{0,3},{5,4},{6,5},{7,6},{4,7},{9,8},{10,9},{11,1... | collective-permute-start | bytes 12296 | tf_op jit(solution)/shard_map/ppermute | solution.py:249
  10.5 0.4 collective-permute-done.6
  10.9 2.3 %collective-permute-start.1 = (s32[4,8,384]{2,1,0:T(8,128)S(1)}, s32[4,8,384]{2,1,0:T(8,128)S(1)}, u32[]{:S(2)}, u32[]{:S(2)}) collective-permute-start(s32[4,8,384]{2,1,0:T(8,128)S(1)} %pad_add_fusion), channel_id=1, source_target_pairs={{4,0},{8,4},{12,8},{16,12},{20,16},{24,20},{28,24},{0,28},{5,1},{9... | collective-permute-start | bytes 147464 | tf_op jit(solution)/shard_map/ppermute | solution.py:249
  13.2 2.6 %collective-permute-start.3 = (f32[3,8,384]{2,1,0:T(8,128)S(1)}, f32[3,8,384]{2,1,0:T(8,128)S(1)}, u32[]{:S(2)}, u32[]{:S(2)}) collective-permute-start(f32[3,8,384]{2,1,0:T(8,128)S(1)} %bitcast.66), channel_id=1, source_target_pairs={{4,0},{8,4},{12,8},{16,12},{20,16},{24,20},{28,24},{0,28},{5,1},{9... | collective-permute-start | bytes 110600 | tf_op jit(solution)/shard_map/ppermute | solution.py:249
  15.8 0.2 bitcast_dynamic-update-slice_fusion.6
  16.4 1.2 collective-permute-done.2
  18.0 3.7 %spread_force.3.partial = f32[3,8,48,128]{3,2,1,0:T(8,128)S(1)} custom-call(s32[2,24]{1,0:T(2,128)S(1)} %pad_add_fusion.6.meta, s32[24,384]{1,0:T(8,128)S(1)} %get-tuple-element.14.key, s32[24,384]{1,0:T(8,128)S(1)} %fusion.12.depth, f32[3,24,384]{2,1,0:T(8,128)S(1)} %pad_maximum_fusion.6.lam), custom_call_target="tpu_custom_call" | custom-call | tf_op jit(solution)/shard_map/spread_force/pallas_call | solution.py:363
  21.7 29.2 %relax_flow.3.field = f32[3,8,48,128]{3,2,1,0:T(8,128)S(1)} custom-call(f32[3,8,32,128]{3,2,1,0:T(8,128)S(1)} %copy-done.1, f32[3,8,32,128]{3,2,1,0:T(8,128)S(1)} %copy-done, f32[3,8,48,128]{3,2,1,0:T(8,128)S(1)} %spread_force.3.partial, f32[7,8,32,128]{3,2,1,0:T(8,128)S(1)} %bitcast_dynamic-update-slice_fusion.terms), custom_call_target="tpu_custom_call" | custom-call | tf_op jit(solution)/shard_map/relax_flow/pallas_call | solution.py:364
  50.9 3.2 %sample_flow.3.sampled = f32[3,24,384]{2,1,0:T(8,128)S(1)} custom-call(s32[2,24]{1,0:T(2,128)S(1)} %pad_add_fusion.6.meta, s32[24,384]{1,0:T(8,128)S(1)} %get-tuple-element.14.key, s32[24,384]{1,0:T(8,128)S(1)} %fusion.12.depth, f32[3,8,48,128]{3,2,1,0:T(8,128)S(1)} %relax_flow.3.field), custom_call_target="tpu_custom_call" | custom-call | tf_op jit(solution)/shard_map/sample_flow/pallas_call | solution.py:366
  54.1 8.8 %fit_body.2 = (f32[3,24,384]{2,1,0:T(8,128)S(1)}, f32[8,128]{1,0:T(8,128)}) custom-call(f32[3,24,384]{2,1,0:T(8,128)S(1)} %sample_flow.3.sampled, f32[3,8,384]{2,1,0:T(8,128)S(1)} %bitcast_convert_fusion.radius, f32[3,24,384]{2,1,0:T(8,128)S(1)} %pad_maximum_fusion.6.lam), custom_call_target="tpu_custom_call" | custom-call | tf_op jit(solution)/shard_map/fit_body/pallas_call | solution.py:367
  62.9 3.7 %spread_force.4.partial = f32[3,8,48,128]{3,2,1,0:T(8,128)S(1)} custom-call(s32[2,24]{1,0:T(2,128)S(1)} %pad_add_fusion.6.meta, s32[24,384]{1,0:T(8,128)S(1)} %get-tuple-element.14.key, s32[24,384]{1,0:T(8,128)S(1)} %fusion.12.depth, f32[3,24,384]{2,1,0:T(8,128)S(1)} %get-tuple-element.5.lam), custom_call_target="tpu_custom_call" | custom-call | tf_op jit(solution)/shard_map/spread_force/pallas_call | solution.py:363
  66.6 30.9 %relax_flow.4.field = f32[3,8,48,128]{3,2,1,0:T(8,128)S(1)} custom-call(f32[3,8,32,128]{3,2,1,0:T(8,128)S(1)} %slice.107.flow, f32[3,8,32,128]{3,2,1,0:T(8,128)S(1)} %copy-done, f32[3,8,48,128]{3,2,1,0:T(8,128)S(1)} %spread_force.4.partial, f32[7,8,32,128]{3,2,1,0:T(8,128)S(1)} %bitcast_dynamic-update-slice_fusion.terms), custom_call_target="tpu_custom_call" | custom-call | tf_op jit(solution)/shard_map/relax_flow/pallas_call | solution.py:364
  97.5 3.2 %sample_flow.4.sampled = f32[3,24,384]{2,1,0:T(8,128)S(1)} custom-call(s32[2,24]{1,0:T(2,128)S(1)} %pad_add_fusion.6.meta, s32[24,384]{1,0:T(8,128)S(1)} %get-tuple-element.14.key, s32[24,384]{1,0:T(8,128)S(1)} %fusion.12.depth, f32[3,8,48,128]{3,2,1,0:T(8,128)S(1)} %relax_flow.4.field), custom_call_target="tpu_custom_call" | custom-call | tf_op jit(solution)/shard_map/sample_flow/pallas_call | solution.py:366
  100.7 7.2 %fit_body.3 = (f32[3,24,384]{2,1,0:T(8,128)S(1)}, f32[8,128]{1,0:T(8,128)}) custom-call(f32[3,24,384]{2,1,0:T(8,128)S(1)} %sample_flow.4.sampled, f32[3,8,384]{2,1,0:T(8,128)S(1)} %bitcast_convert_fusion.radius, f32[3,24,384]{2,1,0:T(8,128)S(1)} %get-tuple-element.5.lam), custom_call_target="tpu_custom_call" | custom-call | tf_op jit(solution)/shard_map/fit_body/pallas_call | solution.py:367
  107.9 3.7 %spread_force.5.partial = f32[3,8,48,128]{3,2,1,0:T(8,128)S(1)} custom-call(s32[2,24]{1,0:T(2,128)S(1)} %pad_add_fusion.6.meta, s32[24,384]{1,0:T(8,128)S(1)} %get-tuple-element.14.key, s32[24,384]{1,0:T(8,128)S(1)} %fusion.12.depth, f32[3,24,384]{2,1,0:T(8,128)S(1)} %get-tuple-element.6.lam), custom_call_target="tpu_custom_call" | custom-call | tf_op jit(solution)/shard_map/spread_force/pallas_call | solution.py:363
  111.6 32.3 %relax_flow.5.field = f32[3,8,48,128]{3,2,1,0:T(8,128)S(1)} custom-call(f32[3,8,32,128]{3,2,1,0:T(8,128)S(1)} %slice.108.flow, f32[3,8,32,128]{3,2,1,0:T(8,128)S(1)} %copy-done, f32[3,8,48,128]{3,2,1,0:T(8,128)S(1)} %spread_force.5.partial, f32[7,8,32,128]{3,2,1,0:T(8,128)S(1)} %bitcast_dynamic-update-slice_fusion.terms), custom_call_target="tpu_custom_call" | custom-call | tf_op jit(solution)/shard_map/relax_flow/pallas_call | solution.py:364
  143.9 3.2 %sample_flow.5.sampled = f32[3,24,384]{2,1,0:T(8,128)S(1)} custom-call(s32[2,24]{1,0:T(2,128)S(1)} %pad_add_fusion.6.meta, s32[24,384]{1,0:T(8,128)S(1)} %get-tuple-element.14.key, s32[24,384]{1,0:T(8,128)S(1)} %fusion.12.depth, f32[3,8,48,128]{3,2,1,0:T(8,128)S(1)} %relax_flow.5.field), custom_call_target="tpu_custom_call" | custom-call | tf_op jit(solution)/shard_map/sample_flow/pallas_call | solution.py:366
  147.1 0.8 slice.109
  147.8 5.0 %fit_last.1 = (f32[3,24,384]{2,1,0:T(8,128)}, f32[8,128]{1,0:T(8,128)S(1)}) custom-call(f32[3,24,384]{2,1,0:T(8,128)S(1)} %sample_flow.5.sampled, f32[3,8,384]{2,1,0:T(8,128)S(1)} %bitcast_convert_fusion.radius, f32[3,24,384]{2,1,0:T(8,128)S(1)} %get-tuple-element.6.lam), custom_call_target="tpu_custom_call" | custom-call | tf_op jit(solution)/shard_map/fit_last/pallas_call | solution.py:367
  152.9 0.7 copy.10
  (51 shorter events, 1.3 us)
Async XLA Ops:
  0.6 8.7 %copy-start.5 = (s32[1,1,8,3]{2,1,3,0:T(1,128)S(1)}, s32[1,1,8,3]{2,1,3,0:T(1,128)}, u32[]{:S(2)}) copy-start(s32[1,1,8,3]{2,1,3,0:T(1,128)} %param.11) | copy-start | bytes 292
  0.6 9.4 %copy-start.3 = (s32[1,1,8,3,384]{4,2,3,1,0:T(8,128)S(1)}, s32[1,1,8,3,384]{4,2,3,1,0:T(8,128)}, u32[]{:S(2)}) copy-start(s32[1,1,8,3,384]{4,2,3,1,0:T(8,128)} %param.12) | copy-start | bytes 110596
  1.4 8.8 %copy-start.2 = (f32[8,32,128]{2,1,0:T(8,128)S(1)}, f32[8,32,128]{2,1,0:T(8,128)}, u32[]{:S(2)}) copy-start(f32[8,32,128]{2,1,0:T(8,128)} %param.9) | copy-start | bytes 393220
  1.4 11.8 %collective-permute-start.5 = (f32[1,32,128]{2,1,0:T(8,128)S(1)}, f32[1,32,128]{2,1,0:T(8,128)S(1)}, u32[]{:S(2)}, u32[]{:S(2)}) collective-permute-start(f32[1,32,128]{2,1,0:T(8,128)S(1)} %get-tuple-element.16), channel_id=1, source_target_pairs={{4,0},{8,4},{12,8},{16,12},{20,16},{24,20},{28,24},{0,28},{5,1},{9... | collective-permute-start | bytes 49160 | tf_op jit(solution)/shard_map/ppermute | solution.py:249
  5.5 5.4 %collective-permute-start.6 = (f32[8,1,128]{2,1,0:T(1,128)S(1)}, f32[8,1,128]{2,1,0:T(1,128)S(1)}, u32[]{:S(2)}, u32[]{:S(2)}) collective-permute-start(f32[8,1,128]{2,1,0:T(1,128)S(1)} %get-tuple-element.18), channel_id=1, source_target_pairs={{0,1},{1,2},{2,3},{3,0},{4,5},{5,6},{6,7},{7,4},{8,9},{9,10},{10,1... | collective-permute-start | bytes 12296 | tf_op jit(solution)/shard_map/ppermute | solution.py:248
  7.1 6.1 %collective-permute-start.7 = (f32[8,1,128]{2,1,0:T(1,128)S(1)}, f32[8,1,128]{2,1,0:T(1,128)S(1)}, u32[]{:S(2)}, u32[]{:S(2)}) collective-permute-start(f32[8,1,128]{2,1,0:T(1,128)S(1)} %get-tuple-element.19), channel_id=1, source_target_pairs={{1,0},{2,1},{3,2},{0,3},{5,4},{6,5},{7,6},{4,7},{9,8},{10,9},{11,1... | collective-permute-start | bytes 12296 | tf_op jit(solution)/shard_map/ppermute | solution.py:249
  9.3 6.5 %collective-permute-start.4 = (f32[1,32,128]{2,1,0:T(8,128)S(1)}, f32[1,32,128]{2,1,0:T(8,128)S(1)}, u32[]{:S(2)}, u32[]{:S(2)}) collective-permute-start(f32[1,32,128]{2,1,0:T(8,128)S(1)} %get-tuple-element.17), channel_id=1, source_target_pairs={{0,4},{4,8},{8,12},{12,16},{16,20},{20,24},{24,28},{28,0},{1,5},{5... | collective-permute-start | bytes 49160 | tf_op jit(solution)/shard_map/ppermute | solution.py:248
  10.2 7.4 %collective-permute-start = (s32[4,8,384]{2,1,0:T(8,128)S(1)}, s32[4,8,384]{2,1,0:T(8,128)S(1)}, u32[]{:S(2)}, u32[]{:S(2)}) collective-permute-start(s32[4,8,384]{2,1,0:T(8,128)S(1)} %pad_add_fusion), channel_id=1, source_target_pairs={{0,4},{4,8},{8,12},{12,16},{16,20},{20,24},{24,28},{28,0},{1,5},{5... | collective-permute-start | bytes 147464 | tf_op jit(solution)/shard_map/ppermute | solution.py:248
  10.3 2.8 %copy-start.4 = (f32[1,1,8,3,384]{4,2,3,1,0:T(8,128)S(1)}, f32[1,1,8,3,384]{4,2,3,1,0:T(8,128)}, u32[]{:S(2)}) copy-start(f32[1,1,8,3,384]{4,2,3,1,0:T(8,128)} %param.10) | copy-start | bytes 110596
  10.9 6.7 %collective-permute-start.1 = (s32[4,8,384]{2,1,0:T(8,128)S(1)}, s32[4,8,384]{2,1,0:T(8,128)S(1)}, u32[]{:S(2)}, u32[]{:S(2)}) collective-permute-start(s32[4,8,384]{2,1,0:T(8,128)S(1)} %pad_add_fusion), channel_id=1, source_target_pairs={{4,0},{8,4},{12,8},{16,12},{20,16},{24,20},{28,24},{0,28},{5,1},{9... | collective-permute-start | bytes 147464 | tf_op jit(solution)/shard_map/ppermute | solution.py:249
  13.2 4.4 %collective-permute-start.2 = (f32[3,8,384]{2,1,0:T(8,128)S(1)}, f32[3,8,384]{2,1,0:T(8,128)S(1)}, u32[]{:S(2)}, u32[]{:S(2)}) collective-permute-start(f32[3,8,384]{2,1,0:T(8,128)S(1)} %bitcast.65), channel_id=1, source_target_pairs={{0,4},{4,8},{8,12},{12,16},{16,20},{20,24},{24,28},{28,0},{1,5},{5... | collective-permute-start | bytes 110600 | tf_op jit(solution)/shard_map/ppermute | solution.py:248
  13.2 4.4 %collective-permute-start.3 = (f32[3,8,384]{2,1,0:T(8,128)S(1)}, f32[3,8,384]{2,1,0:T(8,128)S(1)}, u32[]{:S(2)}, u32[]{:S(2)}) collective-permute-start(f32[3,8,384]{2,1,0:T(8,128)S(1)} %bitcast.66), channel_id=1, source_target_pairs={{4,0},{8,4},{12,8},{16,12},{20,16},{24,20},{28,24},{0,28},{5,1},{9... | collective-permute-start | bytes 110600 | tf_op jit(solution)/shard_map/ppermute | solution.py:249
  18.0 3.7 %copy-start.1 = (f32[3,8,32,128]{3,2,1,0:T(8,128)S(1)}, f32[3,8,32,128]{3,2,1,0:T(8,128)}, u32[]{:S(2)}) copy-start(f32[3,8,32,128]{3,2,1,0:T(8,128)} %flow.1) | copy-start | bytes 1179652
  18.0 3.7 %copy-start = (f32[3,8,32,128]{3,2,1,0:T(8,128)S(1)}, f32[3,8,32,128]{3,2,1,0:T(8,128)}, u32[]{:S(2)}) copy-start(f32[3,8,32,128]{3,2,1,0:T(8,128)} %forcing.5) | copy-start | bytes 1179652
